TPU v7x, 32 devices: a whole 2x2x4 slice. The times are simulated.
32 devices in a mesh: wide: 16 (over z, y, core), narrow: 2 (over x).
Axes of the slice: x: 2, y: 2, z: 4, core: 2. Of those that a mesh axis runs over, the one named last changes fastest.
Arguments:
- positions: float32 [3, 512], P(None, ('wide', 'narrow')), may hold values from 0 to 32
- forces: float32 [27, 512], P(None, ('wide', 'narrow')), may hold values from -6 to 6
- owner: int32 [512, 1], P(('wide', 'narrow')), may hold values from 0 to 15; in each aligned block of 16 rows (0 to 15, 16 to 31, ...) at most 2 rows name the same one
Outputs:
- fraction: float32 [3, 1024], P(None, ('wide', 'narrow'))
- velocities: float32 [27, 1024], P(None, ('wide', 'narrow'))
Inputs may be any that keep to these rules, and one draw needn't show every extreme that they name: Among the 16 swimmers of one device, at most 2 name the same owner; on some devices some owner is named by exactly 2 of them.
All inputs are finite; a program needn't handle non-finite values.
Results may differ from a plain program's by a relative error of at most 0.0003.
Values sent between devices are 32-bit elements; how exact they have to be, the bound alone decides.
No kernel may reach another device: no remote copies, remote signals or barrier semaphores. Data moves between devices by JAX's collectives and lax.ppermute only.
A program may use at most 64 MiB of HBM per device.

v0:
```python
import jax
import jax.numpy as jnp
from jax import lax
from jax.sharding import PartitionSpec as P

BOX = 32


step_time = 0.5
brown_weight = 0.3
tile_edge = 512


def pair_velocity(targets, sources, fields):
    width = sources.shape[1]
    delta = targets[:, :, None] - sources[:, None, :]
    radius = jnp.sqrt(delta[0] * delta[0] + delta[1] * delta[1] + delta[2] * delta[2])
    safe = jnp.maximum(radius, 0.5)
    inverse = 1.0 / safe
    far = radius >= 2.0
    along = jnp.where(
        far, 0.75 * inverse * (1.0 + 2.0 / 3.0 * inverse * inverse), 1.0 - 9.0 / 32.0 * radius
    )
    across = jnp.where(
        far,
        0.75 * inverse * inverse * inverse * (1.0 - 2.0 * inverse * inverse),
        3.0 / 32.0 * inverse,
    )
    split = fields.reshape(3, 9, width)
    tiles = {}
    for first in range(3):
        for second in range(first, 3):
            tiles[first, second] = across * delta[first] * delta[second]
    parts = []
    for first in range(3):
        total = jnp.einsum("ts,ks->kt", along, split[first], precision=lax.Precision.HIGHEST)
        for second in range(3):
            tile = tiles[min(first, second), max(first, second)]
            total = total + jnp.einsum(
                "ts,ks->kt", tile, split[second], precision=lax.Precision.HIGHEST
            )
        parts.append(total)
    return jnp.concatenate(parts, axis=0)


def over_sources(targets, source_pos, source_frc):
    width = source_pos.shape[1]
    edge = tile_edge if width % tile_edge == 0 else width
    if edge == width:
        return pair_velocity(targets, source_pos, source_frc)

    def add_block(index, total):
        begin = index * edge
        place = lax.dynamic_slice_in_dim(source_pos, begin, edge, 1)
        push = lax.dynamic_slice_in_dim(source_frc, begin, edge, 1)
        return total + pair_velocity(targets, place, push)

    start = jnp.zeros((source_frc.shape[0], targets.shape[1]), jnp.float32)
    return lax.fori_loop(0, width // edge, add_block, start)


def body(positions, forces, owner):
    swimmers = positions.shape[1]
    rows = forces.shape[0]
    wide_count = lax.axis_size("wide")
    targets = lax.all_gather(positions, "narrow", axis=1, tiled=True)
    start = jnp.zeros((rows, targets.shape[1]), jnp.float32)
    partial_value = start + over_sources(
        targets,
        lax.all_gather(positions, "wide", axis=1, tiled=True),
        lax.all_gather(forces, "wide", axis=1, tiled=True),
    )
    velocity_own = lax.psum_scatter(partial_value, "narrow", scatter_dimension=1, tiled=True)
    split = velocity_own.reshape(3, 9, swimmers)
    drift = step_time * split[:, 0] + brown_weight * jnp.sum(split[:, 1:], axis=1)
    moved = (positions + drift) / BOX
    capacity = max(2, (2 * swimmers + wide_count - 1) // wide_count)
    per_device = wide_count * capacity
    dest = owner[:, 0]
    local = jnp.arange(swimmers, dtype=jnp.int32)
    same = dest[:, None] == dest[None, :]
    lower = local[None, :] < local[:, None]
    rank = jnp.sum(jnp.where(same & lower, 1, 0), axis=1).astype(jnp.int32)
    slot = dest * capacity + rank
    placing = (slot[:, None] == jnp.arange(per_device, dtype=jnp.int32)[None, :]).astype(
        jnp.float32
    )
    payload = jnp.concatenate([moved, velocity_own], axis=0)
    outgoing = jnp.dot(payload, placing, precision=lax.Precision.HIGHEST)
    send_moved = outgoing[:3]
    send_velocity = outgoing[3:]
    fraction, velocities = (
        lax.all_to_all(send_moved, "wide", split_axis=1, concat_axis=1, tiled=True),
        lax.all_to_all(send_velocity, "wide", split_axis=1, concat_axis=1, tiled=True),
    )
    return (fraction, velocities)


def solution(mesh):
    return jax.shard_map(
        body,
        mesh=mesh,
        in_specs=(
            P(None, ("wide", "narrow")),
            P(None, ("wide", "narrow")),
            P(("wide", "narrow"), None),
        ),
        out_specs=(P(None, ("wide", "narrow")), P(None, ("wide", "narrow"))),
        check_vma=False,
    )
```

profile of v0, /device:TPU:0, one launch (start us, length us, event | category | flops | bytes accessed | tf_op | source)
XLA Modules:
  0.0 99.2 jit_solution(4721349683618981271)
XLA Ops:
  7.2 0.0 reduce-scatter.4.cloned.1.call-start
  7.2 0.0 copy-start
  7.2 23.4 %all-gather.1 = f32[16,16,3]{1,2,0:T(4,128)S(1)} all-gather(f32[1,16,3]{1,2,0:T(4,128)} %bitcast.94), channel_id=1, replica_groups=mesh['wide'=16,'narrow'=2] {'wide'}, dimensions={0}, use_global_device_ids=true | all-gather | bytes 3264 | tf_op jit(solution)/shard_map/all_gather | solution.py:70
  30.6 0.0 copy-done
  30.6 4.3 %all-gather = f32[2,16,3]{1,2,0:T(4,128)S(1)} all-gather(f32[1,16,3]{1,2,0:T(4,128)S(1)} %bitcast.95), channel_id=1, replica_groups=mesh['wide'=16,'narrow'=2] {'narrow'}, dimensions={0}, use_global_device_ids=true | all-gather | bytes 576 | tf_op jit(solution)/shard_map/all_gather | solution.py:66
  35.0 0.1 reshape.28
  35.1 0.1 reshape.26
  35.1 0.1 broadcast_subtract_fusion
  35.2 0.0 copy-start.1
  35.3 0.6 copy-done.1
  35.9 17.5 %all_gather.11 = f32[27,256]{0,1:T(8,128)S(1)} all-gather(f32[27,16]{0,1:T(8,128)S(1)} %copy-done.1), channel_id=1, replica_groups=mesh['wide'=16,'narrow'=2] {'wide'}, dimensions={1}, use_global_device_ids=true | all-gather | bytes 29376 | tf_op jit(solution)/shard_map/all_gather | solution.py:71
  53.4 0.4 fusion.4
  53.8 0.5 fusion.10
  54.3 0.4 fusion.16
  54.6 0.4 convolution_add_fusion.2
  55.0 0.4 convolution_add_fusion.1
  55.4 0.5 fusion
  55.9 0.4 convolution_add_fusion.5
  56.3 0.4 convolution_add_fusion.4
  56.7 0.5 fusion.1
  57.2 0.3 convolution_add_fusion.8
  57.5 0.5 convolution_add_fusion.7
  58.0 0.4 fusion.2
  58.5 0.7 copy.25
  59.2 0.0 reduce-scatter.4.cloned.1.call-update
  59.2 0.0 copy-start.2
  59.2 0.6 copy-done.2
  59.9 0.2 select_reduce_fusion
  60.1 7.8 %reduce-scatter.4.cloned.1.call-done = f32[16,27]{1,0:T(8,128)} async-done(((f32[32,27]{1,0:T(8,128)}), f32[16,27]{1,0:T(8,128)}) %reduce-scatter.4.cloned.1.call-update) | async-done | bytes 1744
  67.9 0.8 copy.26
  68.7 0.2 fusion.29
  68.9 0.7 copy.23
  69.6 5.6 %all-to-all-start = ((f32[3,16,2]{0,2,1:T(2,128)}), f32[3,16,2]{0,2,1:T(2,128)S(1)}, u32[]{:S(2)}, u32[]{:S(2)}) async-start(f32[3,16,2]{0,2,1:T(2,128)} %bitcast.14), calls=%async_computation | async-start | bytes 32768 | tf_op jit(solution)/shard_map/all_to_all | solution.py:93
  75.2 0.7 copy.21
  75.9 5.8 %all-to-all-done = f32[3,16,2]{0,2,1:T(2,128)S(1)} async-done(((f32[3,16,2]{0,2,1:T(2,128)}), f32[3,16,2]{0,2,1:T(2,128)S(1)}, u32[]{:S(2)}, u32[]{:S(2)}) %all-to-all-start) | async-done | bytes 416 | tf_op jit(solution)/shard_map/all_to_all | solution.py:93
  81.7 3.5 %all-to-all-start.1 = ((f32[27,16,2]{0,2,1:T(2,128)}), f32[27,16,2]{0,2,1:T(2,128)S(1)}, u32[]{:S(2)}, u32[]{:S(2)}) async-start(f32[27,16,2]{0,2,1:T(2,128)} %bitcast.16), calls=%async_computation.1 | async-start | bytes 32768 | tf_op jit(solution)/shard_map/all_to_all | solution.py:94
  85.2 0.7 copy.24
  85.9 5.8 %all-to-all-done.1 = f32[27,16,2]{0,2,1:T(2,128)S(1)} async-done(((f32[27,16,2]{0,2,1:T(2,128)}), f32[27,16,2]{0,2,1:T(2,128)S(1)}, u32[]{:S(2)}, u32[]{:S(2)}) %all-to-all-start.1) | async-done | bytes 3488 | tf_op jit(solution)/shard_map/all_to_all | solution.py:94
  91.7 0.7 copy.22
  (11 shorter events, 0.1 us)
Async XLA Ops:
  7.2 60.7 %reduce-scatter.4.cloned.1.call-start = ((), (), s32[]{:S(2)}) async-start(), calls=%async_computation.3 | async-start | bytes 24576
  7.2 23.4 %copy-start = (f32[3,16]{1,0:T(4,128)S(1)}, f32[3,16]{1,0:T(4,128)}, u32[]{:S(2)}) copy-start(f32[3,16]{1,0:T(4,128)} %param.3) | copy-start | bytes 580
  35.2 0.7 copy-start.1
  59.2 0.7 copy-start.2
  69.6 12.1 %all-to-all-start = ((f32[3,16,2]{0,2,1:T(2,128)}), f32[3,16,2]{0,2,1:T(2,128)S(1)}, u32[]{:S(2)}, u32[]{:S(2)}) async-start(f32[3,16,2]{0,2,1:T(2,128)} %bitcast.14), calls=%async_computation | async-start | bytes 32768 | tf_op jit(solution)/shard_map/all_to_all | solution.py:93
  81.7 9.9 %all-to-all-start.1 = ((f32[27,16,2]{0,2,1:T(2,128)}), f32[27,16,2]{0,2,1:T(2,128)S(1)}, u32[]{:S(2)}, u32[]{:S(2)}) async-start(f32[27,16,2]{0,2,1:T(2,128)} %bitcast.16), calls=%async_computation.1 | async-start | bytes 32768 | tf_op jit(solution)/shard_map/all_to_all | solution.py:94
Sparse Core Ops, SparseCore 0:
  59.3 8.4 reduce-scatter.3
where the time goes:
time: 99.6 us; the launch traced here: 99.2 us
  blocking collectives  45.2 us (45%)
  waiting for transfers between devices  19.4 us (19%)
  between operations  14.1 us (14%)
  starting transfers between devices  9.15 us (9%)
  local copies, waits for them, and re-layouts  5.67 us (6%)
  matrix products  5.24 us (5%)
    all_gather x1, blocking collectives, body(): lax.all_gather(positions, 'wide', axis=1, tiled=True)  23.4 us
    all_gather x1, blocking collectives, body(): lax.all_gather(forces, 'wide', axis=1, tiled=True)  17.5 us
    unnamed x2, waiting for transfers between devices  7.81 us
    all_to_all x1, waiting for transfers between devices, body(): lax.all_to_all(send_velocity, 'wide', split_axis=1, concat_axis=1, tiled=...  5.81 us
    all_to_all x1, waiting for transfers between devices, body(): lax.all_to_all(send_moved, 'wide', split_axis=1, concat_axis=1, tiled=True)  5.8 us
    all_to_all x1, starting transfers between devices, body(): lax.all_to_all(send_moved, 'wide', split_axis=1, concat_axis=1, tiled=True)  5.63 us
    all_gather x1, blocking collectives, body(): targets = lax.all_gather(positions, 'narrow', axis=1, tiled=True)  4.33 us
    dot_general x9, matrix products, pair_velocity(): jnp.einsum('ts,ks->kt', tile, split[second], precision=lax.Precision.HIGH...  3.81 us
  transfers between devices with their start and end apart: 3, of which 3 were waited for; matrix products, arithmetic and copies ran while one was open for 2% of the time, Pallas kernels for 0%

commit v1 on v0

v1 whole, which is shorter than its diff:
```python
import functools

import jax
import jax.numpy as jnp
from jax import lax
from jax.experimental import pallas as pl
from jax.experimental.pallas import tpu as pltpu
from jax.sharding import PartitionSpec as P

BOX = 32

step_time = 0.5
brown_weight = 0.3

LANES = 128
WIDTH = 32
CAP = 2


def pack_kernel(positions, forces, owner, out):
    swimmers, features = forces.shape
    small = jnp.concatenate(
        [
            positions[...],
            owner[...].astype(jnp.float32),
            jnp.zeros((4, swimmers), jnp.float32),
        ],
        axis=0,
    )
    small = jnp.concatenate([small, jnp.zeros((8, LANES - swimmers), jnp.float32)], axis=1)
    turned = small.T[:swimmers, :4]
    wide = jnp.concatenate(
        [forces[...], turned, jnp.zeros((swimmers, WIDTH - features - 4), jnp.float32)], axis=1
    )
    rows = swimmers * WIDTH // LANES
    packed = jnp.concatenate(
        [wide[g * rows : (g + 1) * rows] for g in range(LANES // WIDTH)], axis=1
    )
    out[...] = jnp.broadcast_to(packed[None], out.shape)


def halves(value):
    high = value.astype(jnp.bfloat16)
    return high, (value - high.astype(jnp.float32)).astype(jnp.bfloat16)


def move_kernel(rows, narrow_count, features, gathered, fraction, velocities):
    groups = LANES // WIDTH
    count = features // 3
    targets = velocities.shape[1]
    chunks = gathered.shape[0] // LANES
    mine_wide = lax.axis_index("wide").astype(jnp.float32)
    mine_narrow = lax.axis_index("narrow")
    shape = (targets, LANES)
    slot = lax.broadcasted_iota(jnp.int32, shape, 0)
    lane = lax.broadcasted_iota(jnp.int32, shape, 1)
    source = (slot // CAP) * narrow_count + mine_narrow
    device = lane // rows
    within = lane % rows

    def turned(chunk):
        return gathered[pl.ds(chunk * LANES, LANES), :].T

    def field(block, group, index):
        at = group * WIDTH + index
        return block[at : at + 1, :]

    def found(chunk, block):
        here = device + chunk * (LANES // rows) == source
        return [
            here & (field(block, g, features + 3) == mine_wide) for g in range(groups)
        ]

    none = 1 << 20

    def search(chunk, carry):
        first, last = carry
        block = turned(chunk)
        for g, hit in enumerate(found(chunk, block)):
            first = jnp.minimum(first, jnp.where(hit, within + g * rows, none))
            last = jnp.maximum(last, jnp.where(hit, within + g * rows, -1))
        return first, last

    def over(body, start):
        return body(0, start) if chunks == 1 else lax.fori_loop(0, chunks, body, start)

    first, last = over(search, (jnp.full(shape, none), jnp.full(shape, -1)))
    first = jnp.min(first, axis=1, keepdims=True)
    last = jnp.max(last, axis=1, keepdims=True)
    parity = lax.broadcasted_iota(jnp.int32, (targets, 1), 0) % CAP
    chosen = jnp.where(parity == 0, first, jnp.where(last > first, last, none))
    valid = (chosen >= 0) & (chosen < none)

    def collect(chunk, carry):
        block = turned(chunk)
        carry = list(carry)
        for g, hit in enumerate(found(chunk, block)):
            one = hit & (within + g * rows == chosen)
            for c in range(3):
                carry[c] = carry[c] + jnp.where(one, field(block, g, features + c), 0.0)
        return tuple(carry)

    centre = over(collect, (jnp.zeros(shape, jnp.float32),) * 3)
    centre = [jnp.sum(part, axis=1, keepdims=True) for part in centre]

    def pairs(chunk, total):
        block = turned(chunk)
        lefts, rights = [], []
        for g in range(groups):
            delta = [centre[c] - field(block, g, features + c) for c in range(3)]
            square = delta[0] * delta[0] + delta[1] * delta[1] + delta[2] * delta[2]
            root = jnp.minimum(lax.rsqrt(square), 1e18)
            radius = square * root
            inverse = jnp.minimum(root, 2.0)
            far = radius >= 2.0
            second = inverse * inverse
            along = jnp.where(
                far, inverse * (0.75 + 0.5 * second), 1.0 - 9.0 / 32.0 * radius
            )
            across = inverse * jnp.where(far, second * (0.75 - 1.5 * second), 3.0 / 32.0)
            scaled = [across * delta[c] for c in range(3)]
            lefts.append(
                jnp.concatenate(
                    [along]
                    + [scaled[a] * delta[b] for a in range(3) for b in range(a, 3)],
                    axis=0,
                )
            )
            rights.append(block[g * WIDTH : (g + 1) * WIDTH, :])
        left = jnp.concatenate(lefts, axis=1)
        right = jnp.concatenate(rights, axis=1)
        left_high, left_low = halves(left)
        right = jnp.concatenate(halves(right), axis=0)

        def dot(part):
            return lax.dot_general(
                part, right, (((1,), (1,)), ((), ())), preferred_element_type=jnp.float32
            )

        return total + (dot(left_high) + dot(left_low))

    total = over(pairs, jnp.zeros((7 * targets, 2 * WIDTH), jnp.float32))
    total = total[:, :WIDTH] + total[:, WIDTH:]
    parts = [total[m * targets : (m + 1) * targets] for m in range(7)]
    tile = {}
    at = 1
    for a in range(3):
        for b in range(a, 3):
            tile[a, b] = tile[b, a] = parts[at]
            at += 1
    outs = []
    for c in range(3):
        value = parts[0][:, c * count : (c + 1) * count]
        for e in range(3):
            value = value + tile[c, e][:, e * count : (e + 1) * count]
        outs.append(value)
    wide = jnp.concatenate(
        outs + centre + [jnp.zeros((targets, LANES - features - 3), jnp.float32)], axis=1
    )
    wide = jnp.where(valid, wide, 0.0).T
    velocity = wide[:features]
    velocities[...] = velocity
    for c in range(3):
        lead = velocity[c * count : c * count + 1]
        rest = jnp.sum(velocity[c * count + 1 : (c + 1) * count], axis=0, keepdims=True)
        drift = step_time * lead + brown_weight * rest
        fraction[c : c + 1, :] = (wide[features + c : features + c + 1] + drift) / BOX


def body(positions, forces, owner):
    swimmers = positions.shape[1]
    features = forces.shape[0]
    wide_count = lax.axis_size("wide")
    narrow_count = lax.axis_size("narrow")
    devices = wide_count * narrow_count
    rows = swimmers * WIDTH // LANES
    vmem = pl.BlockSpec(memory_space=pltpu.VMEM)
    packed = pl.pallas_call(
        pack_kernel,
        out_shape=jax.ShapeDtypeStruct((devices, rows, LANES), jnp.float32),
        in_specs=[vmem] * 3,
        out_specs=vmem,
    )(positions, forces.T, owner.reshape(1, swimmers))
    gathered = lax.all_to_all(packed, ("wide", "narrow"), split_axis=0, concat_axis=0)
    gathered = gathered.reshape(devices * rows, LANES)
    slots = wide_count * CAP
    return pl.pallas_call(
        functools.partial(move_kernel, rows, narrow_count, features),
        out_shape=(
            jax.ShapeDtypeStruct((3, slots), jnp.float32),
            jax.ShapeDtypeStruct((features, slots), jnp.float32),
        ),
        in_specs=[vmem],
        out_specs=(vmem, vmem),
    )(gathered)


def solution(mesh):
    return jax.shard_map(
        body,
        mesh=mesh,
        in_specs=(
            P(None, ("wide", "narrow")),
            P(None, ("wide", "narrow")),
            P(("wide", "narrow"), None),
        ),
        out_specs=(P(None, ("wide", "narrow")), P(None, ("wide", "narrow"))),
        check_vma=False,
    )
```

time: 99.6 us -> 19.7 us (0.20)
  blocking collectives: 45.2 us -> 15 us
  waiting for transfers between devices: 19.4 us -> 0 us
  between operations: 14.1 us -> 0.63 us
  starting transfers between devices: 9.15 us -> 0 us
  local copies, waits for them, and re-layouts: 5.67 us -> 0 us
  matrix products: 5.24 us -> 0 us
  Pallas kernels: 0 us -> 3.83 us
    all_gather x3 -> x0, blocking collectives: 45.2 us -> none  [the longest x1 23.4 us: body(): lax.all_gather(positions, 'wide', axis=1, tiled=True)]
    all_to_all x0 -> x1, blocking collectives: none -> 15 us  [body(): lax.all_to_all(packed, ('wide', 'narrow'), split_axis=0, concat_axis=0)]
    all_to_all x2 -> x0, waiting for transfers between devices: 11.6 us -> none  [the longest x1 5.81 us: body(): lax.all_to_all(send_velocity, 'wide', split_axis=1, concat_axis=1, tiled=...]
    all_to_all x2 -> x0, starting transfers between devices: 9.11 us -> none  [the longest x1 5.63 us: body(): lax.all_to_all(send_moved, 'wide', split_axis=1, concat_axis=1, tiled=True)]
    unnamed x2 -> x0, waiting for transfers between devices: 7.81 us -> none
    dot_general x13 -> x0, matrix products: 5.24 us -> none  [the longest x9 3.81 us: pair_velocity(): jnp.einsum('ts,ks->kt', tile, split[second], precision=lax.Precision.HIGH...]
    pallas_call x0 -> x2, Pallas kernels: none -> 3.83 us  [the longest x1 2.29 us: body(): pl.pallas_call(functools.partial(move_kernel, rows, narrow_count, feature...]
    unnamed x11 -> x0, local copies, waits for them, and re-layouts: 3.62 us -> none
  transfers between devices with their start and end apart: 3 -> 0, of which waited for: 3 -> 0; matrix products, arithmetic and copies ran while one was open for 2% -> 0% of each run, Pallas kernels for 0% -> 0%
where the time goes in v1:
time: 19.7 us; the launch traced here: 19.5 us
  blocking collectives  15 us (76%)
  Pallas kernels  3.83 us (19%)
  between operations  0.63 us (3%)
    all_to_all x1, blocking collectives, body(): lax.all_to_all(packed, ('wide', 'narrow'), split_axis=0, concat_axis=0)  15 us
    pallas_call x1, Pallas kernels, body(): pl.pallas_call(functools.partial(move_kernel, rows, narrow_count, feature...  2.29 us
    pallas_call x1, Pallas kernels, body(): pl.pallas_call(pack_kernel, out_shape=jax.ShapeDtypeStruct((devices, rows...  1.54 us

profile of v1, /device:TPU:0, one launch (start us, length us, event | category | flops | bytes accessed | tf_op | source)
XLA Modules:
  0.0 19.5 jit_solution(840528800038797107)
XLA Ops:
  0.6 1.5 %shard_map.50 = f32[32,4,128]{2,1,0:T(4,128)} custom-call(f32[3,16]{1,0:T(4,128)} %positions.1, f32[16,27]{1,0:T(8,128)} %bitcast.4, s32[1,16]{1,0:T(1,128)} %bitcast.5), custom_call_target="tpu_custom_call" | custom-call | tf_op jit(solution)/shard_map/pallas_call | solution.py:178
  2.2 15.0 %all_to_all.5 = f32[32,4,128]{2,1,0:T(4,128)} all-to-all(f32[32,4,128]{2,1,0:T(4,128)} %shard_map.50), channel_id=1, replica_groups=mesh['wide'=16,'narrow'=2] {'wide','narrow'}, dimensions={0} | all-to-all | bytes 131072 | tf_op jit(solution)/shard_map/all_to_all | solution.py:184
  17.2 2.3 %shard_map.51 = (f32[3,32]{1,0:T(4,128)}, f32[27,32]{1,0:T(8,128)}) custom-call(f32[128,128]{1,0:T(8,128)} %bitcast.3), custom_call_target="tpu_custom_call" | custom-call | tf_op jit(solution)/shard_map/pallas_call | solution.py:187

commit v2 on v1

--- a/solution.py
+++ b/solution.py
@@ -180,6 +180,7 @@
         out_shape=jax.ShapeDtypeStruct((devices, rows, LANES), jnp.float32),
         in_specs=[vmem] * 3,
         out_specs=vmem,
+        compiler_params=pltpu.CompilerParams(vmem_limit_bytes=4 << 20),
     )(positions, forces.T, owner.reshape(1, swimmers))
     gathered = lax.all_to_all(packed, ("wide", "narrow"), split_axis=0, concat_axis=0)
     gathered = gathered.reshape(devices * rows, LANES)
@@ -192,6 +193,7 @@
         ),
         in_specs=[vmem],
         out_specs=(vmem, vmem),
+        compiler_params=pltpu.CompilerParams(vmem_limit_bytes=16 << 20),
     )(gathered)
 
 

time: 19.7 us -> 18.7 us (0.949)
  Pallas kernels: 3.83 us -> 1.67 us
  local copies, waits for them, and re-layouts: 0 us -> 1.37 us
  blocking collectives: 15 us -> 14.7 us
    unnamed x0 -> x6, local copies, waits for them, and re-layouts: none -> 1.37 us
    pallas_call x1, Pallas kernels: 1.54 us -> 0.22 us  [body(): pl.pallas_call(pack_kernel, out_shape=jax.ShapeDtypeStruct((devices, rows...]
    pallas_call x1, Pallas kernels: 2.29 us -> 1.45 us  [body(): pl.pallas_call(functools.partial(move_kernel, rows, narrow_count, feature...]
    all_to_all x1, blocking collectives: 15 us -> 14.7 us  [body(): lax.all_to_all(packed, ('wide', 'narrow'), split_axis=0, concat_axis=0)]
where the time goes in v2:
time: 18.7 us; the launch traced here: 18.4 us
  blocking collectives  14.7 us (79%)
  Pallas kernels  1.67 us (9%)
  local copies, waits for them, and re-layouts  1.37 us (7%)
  between operations  0.65 us (3%)
    all_to_all x1, blocking collectives, body(): lax.all_to_all(packed, ('wide', 'narrow'), split_axis=0, concat_axis=0)  14.7 us
    pallas_call x1, Pallas kernels, body(): pl.pallas_call(functools.partial(move_kernel, rows, narrow_count, feature...  1.45 us
    unnamed x6, local copies, waits for them, and re-layouts  1.37 us

profile of v2, /device:TPU:0, one launch (start us, length us, event | category | flops | bytes accessed | tf_op | source)
XLA Modules:
  0.0 18.4 jit_solution(6752836450295918886)
XLA Ops:
  0.6 0.0 copy-start.1
  0.6 0.0 copy-start.2
  0.6 0.7 %copy-done.1 = f32[3,16]{1,0:T(4,128)S(1)} copy-done((f32[3,16]{1,0:T(4,128)S(1)}, f32[3,16]{1,0:T(4,128)}, u32[]{:S(2)}) %copy-start.1) | copy-done | bytes 216
  1.3 0.0 copy-done.2
  1.3 0.0 copy-start
  1.3 0.7 %copy-done = f32[27,16]{0,1:T(8,128)S(1)} copy-done((f32[27,16]{0,1:T(8,128)S(1)}, f32[27,16]{0,1:T(8,128)}, u32[]{:S(2)}) %copy-start) | copy-done | bytes 1752
  2.0 0.2 %shard_map.50 = f32[32,4,128]{2,1,0:T(4,128)S(1)} custom-call(f32[3,16]{1,0:T(4,128)S(1)} %copy-done.1, f32[16,27]{1,0:T(8,128)S(1)} %bitcast.4, s32[1,16]{1,0:T(1,128)S(1)} %bitcast.5), custom_call_target="tpu_custom_call" | custom-call | tf_op jit(solution)/shard_map/pallas_call | solution.py:178
  2.2 14.7 %all_to_all.5 = f32[32,4,128]{2,1,0:T(4,128)S(1)} all-to-all(f32[32,4,128]{2,1,0:T(4,128)S(1)} %shard_map.50), channel_id=1, replica_groups=mesh['wide'=16,'narrow'=2] {'wide','narrow'}, dimensions={0} | all-to-all | bytes 131072 | tf_op jit(solution)/shard_map/all_to_all | solution.py:185
  16.9 1.5 %shard_map.51 = (f32[3,32]{1,0:T(4,128)}, f32[27,32]{1,0:T(8,128)}) custom-call(f32[128,128]{1,0:T(8,128)S(1)} %bitcast.3), custom_call_target="tpu_custom_call" | custom-call | tf_op jit(solution)/shard_map/pallas_call | solution.py:188
Async XLA Ops:
  0.6 0.7 %copy-start.1 = (f32[3,16]{1,0:T(4,128)S(1)}, f32[3,16]{1,0:T(4,128)}, u32[]{:S(2)}) copy-start(f32[3,16]{1,0:T(4,128)} %positions.1) | copy-start | bytes 580
  0.6 0.7 %copy-start.2 = (s32[16,1]{0,1:T(1,128)S(1)}, s32[16,1]{0,1:T(1,128)}, u32[]{:S(2)}) copy-start(s32[16,1]{0,1:T(1,128)} %param.5) | copy-start | bytes 196
  1.3 0.7 %copy-start = (f32[27,16]{0,1:T(8,128)S(1)}, f32[27,16]{0,1:T(8,128)}, u32[]{:S(2)}) copy-start(f32[27,16]{0,1:T(8,128)} %param.4) | copy-start | bytes 5188

commit v3 on v2

--- a/solution.py
+++ b/solution.py
@@ -17,18 +17,11 @@
 CAP = 2
 
 
-def pack_kernel(positions, forces, owner, out):
+def pack_kernel(small, forces, out):
     swimmers, features = forces.shape
-    small = jnp.concatenate(
-        [
-            positions[...],
-            owner[...].astype(jnp.float32),
-            jnp.zeros((4, swimmers), jnp.float32),
-        ],
-        axis=0,
-    )
-    small = jnp.concatenate([small, jnp.zeros((8, LANES - swimmers), jnp.float32)], axis=1)
-    turned = small.T[:swimmers, :4]
+    square = jnp.concatenate([small[...], jnp.zeros((4, swimmers), jnp.float32)], axis=0)
+    square = jnp.concatenate([square, jnp.zeros((8, LANES - swimmers), jnp.float32)], axis=1)
+    turned = square.T[:swimmers, :4]
     wide = jnp.concatenate(
         [forces[...], turned, jnp.zeros((swimmers, WIDTH - features - 4), jnp.float32)], axis=1
     )
@@ -54,7 +47,7 @@
     shape = (targets, LANES)
     slot = lax.broadcasted_iota(jnp.int32, shape, 0)
     lane = lax.broadcasted_iota(jnp.int32, shape, 1)
-    source = (slot // CAP) * narrow_count + mine_narrow
+    source = gathered.shape[0] // rows - 1 - (slot // CAP) * narrow_count - mine_narrow
     device = lane // rows
     within = lane % rows
 
@@ -175,14 +168,18 @@
     devices = wide_count * narrow_count
     rows = swimmers * WIDTH // LANES
     vmem = pl.BlockSpec(memory_space=pltpu.VMEM)
+    small = jnp.concatenate([positions.T, owner.astype(jnp.float32)], axis=1).T
     packed = pl.pallas_call(
         pack_kernel,
         out_shape=jax.ShapeDtypeStruct((devices, rows, LANES), jnp.float32),
-        in_specs=[vmem] * 3,
+        in_specs=[vmem] * 2,
         out_specs=vmem,
         compiler_params=pltpu.CompilerParams(vmem_limit_bytes=4 << 20),
-    )(positions, forces.T, owner.reshape(1, swimmers))
-    gathered = lax.all_to_all(packed, ("wide", "narrow"), split_axis=0, concat_axis=0)
+    )(small, forces.T)
+    order = list(range(devices))[::-1]
+    gathered = lax.all_to_all(
+        packed, ("wide", "narrow"), split_axis=0, concat_axis=0, axis_index_groups=[order]
+    )
     gathered = gathered.reshape(devices * rows, LANES)
     slots = wide_count * CAP
     return pl.pallas_call(

time: 18.7 us -> 17.4 us (0.930)
  local copies, waits for them, and re-layouts: 1.37 us -> 0.02 us
  other arithmetic: 0 us -> 0.68 us
  blocking collectives: 14.7 us -> 14.2 us
    unnamed x6 -> x4, local copies, waits for them, and re-layouts: 1.37 us -> 0.02 us
    convert_element_type x0 -> x1, other arithmetic: none -> 0.67 us  [body(): small = jnp.concatenate([positions.T, owner.astype(jnp.float32)], axis=1).T]
    all_to_all x1, blocking collectives: 14.7 us -> 14.2 us  [body(): lax.all_to_all(packed, ('wide', 'narrow'), split_axis=0, concat_axis=0, a...]
where the time goes in v3:
time: 17.4 us; the launch traced here: 17.2 us
  blocking collectives  14.2 us (82%)
  Pallas kernels  1.67 us (10%)
  other arithmetic  0.68 us (4%)
  between operations  0.65 us (4%)
    all_to_all x1, blocking collectives, body(): lax.all_to_all(packed, ('wide', 'narrow'), split_axis=0, concat_axis=0, a...  14.2 us
    pallas_call x1, Pallas kernels, body(): pl.pallas_call(functools.partial(move_kernel, rows, narrow_count, feature...  1.45 us
    convert_element_type x1, other arithmetic, body(): small = jnp.concatenate([positions.T, owner.astype(jnp.float32)], axis=1).T  0.67 us

profile of v3, /device:TPU:0, one launch (start us, length us, event | category | flops | bytes accessed | tf_op | source)
XLA Modules:
  0.0 17.2 jit_solution(6955156854188835244)
XLA Ops:
  0.6 0.0 copy-start.1
  0.6 0.0 copy-start
  0.6 0.7 %convert_element_type.3 = f32[16,1]{0,1:T(1,128)S(1)} convert(s32[16,1]{0,1:T(1,128)} %param.5) | non-fusion elementwise | flops 16 | bytes 128 | tf_op jit(solution)/shard_map/convert_element_type | solution.py:171
  1.3 0.0 copy-done.1
  1.3 0.0 copy-done
  1.3 0.2 %shard_map.50 = f32[32,4,128]{2,1,0:T(4,128)S(1)} custom-call(f32[4,16]{1,0:T(4,128)S(1)} %maximum_bitcast_fusion.small, f32[16,27]{1,0:T(8,128)S(1)} %bitcast.6), custom_call_target="tpu_custom_call" | custom-call | tf_op jit(solution)/shard_map/pallas_call | solution.py:172
  1.6 14.2 %all_to_all.5 = f32[32,4,128]{2,1,0:T(4,128)S(1)} all-to-all(f32[32,4,128]{2,1,0:T(4,128)S(1)} %shard_map.50), channel_id=1, replica_groups={{31,30,29,28,27,26,25,24,23,22,21,20,19,18,17,16,15,14,13,12,11,10,9,8,..., dimensions={0} | all-to-all | bytes 131072 | tf_op jit(solution)/shard_map/all_to_all | solution.py:180
  15.8 1.5 %shard_map.51 = (f32[3,32]{1,0:T(4,128)}, f32[27,32]{1,0:T(8,128)}) custom-call(f32[128,128]{1,0:T(8,128)S(1)} %bitcast.5), custom_call_target="tpu_custom_call" | custom-call | tf_op jit(solution)/shard_map/pallas_call | solution.py:185
  (1 shorter events, 0.0 us)
Async XLA Ops:
  0.6 0.7 %copy-start.1 = (f32[3,16]{1,0:T(4,128)S(1)}, f32[3,16]{1,0:T(4,128)}, u32[]{:S(2)}) copy-start(f32[3,16]{1,0:T(4,128)} %param.3) | copy-start | bytes 580
  0.6 0.7 %copy-start = (f32[27,16]{0,1:T(8,128)S(1)}, f32[27,16]{0,1:T(8,128)}, u32[]{:S(2)}) copy-start(f32[27,16]{0,1:T(8,128)} %param.4) | copy-start | bytes 5188

commit v4 on v3

--- a/solution.py
+++ b/solution.py
@@ -19,16 +19,37 @@
 
 def pack_kernel(small, forces, out):
     swimmers, features = forces.shape
-    square = jnp.concatenate([small[...], jnp.zeros((4, swimmers), jnp.float32)], axis=0)
-    square = jnp.concatenate([square, jnp.zeros((8, LANES - swimmers), jnp.float32)], axis=1)
-    turned = square.T[:swimmers, :4]
-    wide = jnp.concatenate(
-        [forces[...], turned, jnp.zeros((swimmers, WIDTH - features - 4), jnp.float32)], axis=1
-    )
     rows = swimmers * WIDTH // LANES
-    packed = jnp.concatenate(
-        [wide[g * rows : (g + 1) * rows] for g in range(LANES // WIDTH)], axis=1
-    )
+    square = jnp.concatenate(
+        [
+            jnp.zeros((features, swimmers), jnp.float32),
+            small[...],
+            jnp.zeros((WIDTH - features - 4, swimmers), jnp.float32),
+        ],
+        axis=0,
+    )
+    square = jnp.concatenate(
+        [square, jnp.full((WIDTH, LANES - swimmers), -1.0, jnp.float32)], axis=1
+    )
+    row = square[features + 3 : features + 4, :]
+    before = pltpu.roll(jnp.broadcast_to(row, (swimmers, LANES)), 1, 1, stride=1, stride_axis=0)
+    earlier = lax.broadcasted_iota(jnp.int32, before.shape, 0) < lax.broadcasted_iota(
+        jnp.int32, before.shape, 1
+    )
+    rank = jnp.sum(jnp.where((before == row) & earlier, 1.0, 0.0), axis=0, keepdims=True)
+    at = lax.broadcasted_iota(jnp.int32, square.shape, 0)
+    square = jnp.where(at == features + 4, rank, square)
+    turned = jnp.concatenate(
+        [square.T[:swimmers], jnp.zeros((swimmers, LANES - WIDTH), jnp.float32)], axis=1
+    )
+    first = jnp.concatenate(
+        [forces[...], jnp.zeros((swimmers, LANES - features), jnp.float32)], axis=1
+    )
+    lane = lax.broadcasted_iota(jnp.int32, first.shape, 1)
+    wide = jnp.where(lane < features, first, turned)
+    packed = wide[:rows]
+    for g in range(1, LANES // WIDTH):
+        packed = packed + pltpu.roll(wide, g * WIDTH, 1)[g * rows : (g + 1) * rows]
     out[...] = jnp.broadcast_to(packed[None], out.shape)
 
 
@@ -49,7 +70,7 @@
     lane = lax.broadcasted_iota(jnp.int32, shape, 1)
     source = gathered.shape[0] // rows - 1 - (slot // CAP) * narrow_count - mine_narrow
     device = lane // rows
-    within = lane % rows
+    rank = (slot % CAP).astype(jnp.float32)
 
     def turned(chunk):
         return gathered[pl.ds(chunk * LANES, LANES), :].T
@@ -58,43 +79,27 @@
         at = group * WIDTH + index
         return block[at : at + 1, :]
 
-    def found(chunk, block):
-        here = device + chunk * (LANES // rows) == source
-        return [
-            here & (field(block, g, features + 3) == mine_wide) for g in range(groups)
-        ]
-
-    none = 1 << 20
-
-    def search(chunk, carry):
-        first, last = carry
-        block = turned(chunk)
-        for g, hit in enumerate(found(chunk, block)):
-            first = jnp.minimum(first, jnp.where(hit, within + g * rows, none))
-            last = jnp.maximum(last, jnp.where(hit, within + g * rows, -1))
-        return first, last
-
     def over(body, start):
         return body(0, start) if chunks == 1 else lax.fori_loop(0, chunks, body, start)
 
-    first, last = over(search, (jnp.full(shape, none), jnp.full(shape, -1)))
-    first = jnp.min(first, axis=1, keepdims=True)
-    last = jnp.max(last, axis=1, keepdims=True)
-    parity = lax.broadcasted_iota(jnp.int32, (targets, 1), 0) % CAP
-    chosen = jnp.where(parity == 0, first, jnp.where(last > first, last, none))
-    valid = (chosen >= 0) & (chosen < none)
-
     def collect(chunk, carry):
         block = turned(chunk)
+        here = device + chunk * (LANES // rows) == source
         carry = list(carry)
-        for g, hit in enumerate(found(chunk, block)):
-            one = hit & (within + g * rows == chosen)
+        for g in range(groups):
+            hit = (
+                here
+                & (field(block, g, features + 3) == mine_wide)
+                & (field(block, g, features + 4) == rank)
+            )
             for c in range(3):
-                carry[c] = carry[c] + jnp.where(one, field(block, g, features + c), 0.0)
+                carry[c] = carry[c] + jnp.where(hit, field(block, g, features + c), 0.0)
+            carry[3] = carry[3] + jnp.where(hit, 1.0, 0.0)
         return tuple(carry)
 
-    centre = over(collect, (jnp.zeros(shape, jnp.float32),) * 3)
+    centre = over(collect, (jnp.zeros(shape, jnp.float32),) * 4)
     centre = [jnp.sum(part, axis=1, keepdims=True) for part in centre]
+    valid = centre.pop() > 0.0
 
     def pairs(chunk, total):
         block = turned(chunk)
@@ -112,10 +117,10 @@
             )
             across = inverse * jnp.where(far, second * (0.75 - 1.5 * second), 3.0 / 32.0)
             scaled = [across * delta[c] for c in range(3)]
+            tiles = [scaled[a] * delta[b] for a in range(3) for b in range(a, 3)]
             lefts.append(
                 jnp.concatenate(
-                    [along]
-                    + [scaled[a] * delta[b] for a in range(3) for b in range(a, 3)],
+                    [along + tile if k in (0, 3, 5) else tile for k, tile in enumerate(tiles)],
                     axis=0,
                 )
             )
@@ -127,30 +132,28 @@
 
         def dot(part):
             return lax.dot_general(
-                part, right, (((1,), (1,)), ((), ())), preferred_element_type=jnp.float32
+                right, part, (((1,), (1,)), ((), ())), preferred_element_type=jnp.float32
             )
 
         return total + (dot(left_high) + dot(left_low))
 
-    total = over(pairs, jnp.zeros((7 * targets, 2 * WIDTH), jnp.float32))
-    total = total[:, :WIDTH] + total[:, WIDTH:]
-    parts = [total[m * targets : (m + 1) * targets] for m in range(7)]
+    total = over(pairs, jnp.zeros((2 * WIDTH, 6 * targets), jnp.float32))
+    total = total[:WIDTH] + total[WIDTH:]
+    parts = [total[:, m * targets : (m + 1) * targets] for m in range(6)]
     tile = {}
-    at = 1
+    at = 0
     for a in range(3):
         for b in range(a, 3):
             tile[a, b] = tile[b, a] = parts[at]
             at += 1
     outs = []
     for c in range(3):
-        value = parts[0][:, c * count : (c + 1) * count]
-        for e in range(3):
-            value = value + tile[c, e][:, e * count : (e + 1) * count]
-        outs.append(value)
-    wide = jnp.concatenate(
-        outs + centre + [jnp.zeros((targets, LANES - features - 3), jnp.float32)], axis=1
-    )
-    wide = jnp.where(valid, wide, 0.0).T
+        outs.append(sum(tile[c, e][e * count : (e + 1) * count] for e in range(3)))
+    rows_of = jnp.concatenate(
+        centre + [jnp.where(valid, 1.0, 0.0), jnp.zeros((targets, LANES - 4), jnp.float32)], axis=1
+    ).T[:8, :targets]
+    there = rows_of[3:4] > 0.0
+    wide = jnp.where(there, jnp.concatenate(outs + [rows_of[:3]], axis=0), 0.0)
     velocity = wide[:features]
     velocities[...] = velocity
     for c in range(3):

time: 17.4 us -> 17.2 us (0.989)
  Pallas kernels: 1.67 us -> 1.49 us
    pallas_call x1, Pallas kernels: 1.45 us -> 1.26 us  [body(): pl.pallas_call(functools.partial(move_kernel, rows, narrow_count, feature...]
where the time goes in v4:
time: 17.2 us; the launch traced here: 17.1 us
  blocking collectives  14.2 us (83%)
  Pallas kernels  1.49 us (9%)
  other arithmetic  0.68 us (4%)
  between operations  0.65 us (4%)
    all_to_all x1, blocking collectives, body(): lax.all_to_all(packed, ('wide', 'narrow'), split_axis=0, concat_axis=0, a...  14.2 us
    pallas_call x1, Pallas kernels, body(): pl.pallas_call(functools.partial(move_kernel, rows, narrow_count, feature...  1.26 us
    convert_element_type x1, other arithmetic, body(): small = jnp.concatenate([positions.T, owner.astype(jnp.float32)], axis=1).T  0.67 us

profile of v4, /device:TPU:0, one launch (start us, length us, event | category | flops | bytes accessed | tf_op | source)
XLA Modules:
  0.0 17.1 jit_solution(13423734681999998897)
XLA Ops:
  0.6 0.0 copy-start.1
  0.6 0.0 copy-start
  0.6 0.7 %convert_element_type.3 = f32[16,1]{0,1:T(1,128)S(1)} convert(s32[16,1]{0,1:T(1,128)} %param.5) | non-fusion elementwise | flops 16 | bytes 128 | tf_op jit(solution)/shard_map/convert_element_type | solution.py:174
  1.3 0.0 copy-done.1
  1.3 0.0 copy-done
  1.3 0.2 %shard_map.50 = f32[32,4,128]{2,1,0:T(4,128)S(1)} custom-call(f32[4,16]{1,0:T(4,128)S(1)} %maximum_bitcast_fusion.small, f32[16,27]{1,0:T(8,128)S(1)} %bitcast.6), custom_call_target="tpu_custom_call" | custom-call | tf_op jit(solution)/shard_map/pallas_call | solution.py:175
  1.6 14.2 %all_to_all.5 = f32[32,4,128]{2,1,0:T(4,128)S(1)} all-to-all(f32[32,4,128]{2,1,0:T(4,128)S(1)} %shard_map.50), channel_id=1, replica_groups={{31,30,29,28,27,26,25,24,23,22,21,20,19,18,17,16,15,14,13,12,11,10,9,8,..., dimensions={0} | all-to-all | bytes 131072 | tf_op jit(solution)/shard_map/all_to_all | solution.py:183
  15.8 1.3 %shard_map.51 = (f32[3,32]{1,0:T(4,128)}, f32[27,32]{1,0:T(8,128)}) custom-call(f32[128,128]{1,0:T(8,128)S(1)} %bitcast.5), custom_call_target="tpu_custom_call" | custom-call | tf_op jit(solution)/shard_map/pallas_call | solution.py:188
  (1 shorter events, 0.0 us)
Async XLA Ops:
  0.6 0.7 %copy-start.1 = (f32[3,16]{1,0:T(4,128)S(1)}, f32[3,16]{1,0:T(4,128)}, u32[]{:S(2)}) copy-start(f32[3,16]{1,0:T(4,128)} %param.3) | copy-start | bytes 580
  0.6 0.7 %copy-start = (f32[27,16]{0,1:T(8,128)S(1)}, f32[27,16]{0,1:T(8,128)}, u32[]{:S(2)}) copy-start(f32[27,16]{0,1:T(8,128)} %param.4) | copy-start | bytes 5188

commit v5 on v4

--- a/solution.py
+++ b/solution.py
@@ -58,22 +58,28 @@
     return high, (value - high.astype(jnp.float32)).astype(jnp.bfloat16)
 
 
-def move_kernel(rows, narrow_count, features, gathered, fraction, velocities):
+def move_kernel(rows, narrow_count, features, own, other, fraction, velocities):
     groups = LANES // WIDTH
     count = features // 3
     targets = velocities.shape[1]
-    chunks = gathered.shape[0] // LANES
-    mine_wide = lax.axis_index("wide").astype(jnp.float32)
+    half = LANES // 2
+    chunks = own.shape[0] // half
+    side = own.shape[0] // rows
+    index = lax.axis_index("wide")
+    mine_wide = index.astype(jnp.float32)
     mine_narrow = lax.axis_index("narrow")
     shape = (targets, LANES)
     slot = lax.broadcasted_iota(jnp.int32, shape, 0)
     lane = lax.broadcasted_iota(jnp.int32, shape, 1)
-    source = gathered.shape[0] // rows - 1 - (slot // CAP) * narrow_count - mine_narrow
-    device = lane // rows
+    giver = slot // CAP
+    source = side - 1 - giver // 2 * narrow_count - mine_narrow
+    source = source + jnp.where(giver % 2 == index % 2, 0, side)
+    device = lane // half * side + lane % half // rows
     rank = (slot % CAP).astype(jnp.float32)
 
     def turned(chunk):
-        return gathered[pl.ds(chunk * LANES, LANES), :].T
+        at = pl.ds(chunk * half, half)
+        return jnp.concatenate([own[at, :], other[at, :]], axis=0).T
 
     def field(block, group, index):
         at = group * WIDTH + index
@@ -84,7 +90,7 @@
 
     def collect(chunk, carry):
         block = turned(chunk)
-        here = device + chunk * (LANES // rows) == source
+        here = device + chunk * (half // rows) == source
         carry = list(carry)
         for g in range(groups):
             hit = (
@@ -174,16 +180,24 @@
     small = jnp.concatenate([positions.T, owner.astype(jnp.float32)], axis=1).T
     packed = pl.pallas_call(
         pack_kernel,
-        out_shape=jax.ShapeDtypeStruct((devices, rows, LANES), jnp.float32),
+        out_shape=jax.ShapeDtypeStruct((devices // 2, rows, LANES), jnp.float32),
         in_specs=[vmem] * 2,
         out_specs=vmem,
         compiler_params=pltpu.CompilerParams(vmem_limit_bytes=4 << 20),
     )(small, forces.T)
-    order = list(range(devices))[::-1]
-    gathered = lax.all_to_all(
-        packed, ("wide", "narrow"), split_axis=0, concat_axis=0, axis_index_groups=[order]
-    )
-    gathered = gathered.reshape(devices * rows, LANES)
+    order = [
+        [w * narrow_count + n for w in range(parity, wide_count, 2) for n in range(narrow_count)]
+        for parity in range(2)
+    ]
+    own = lax.all_to_all(
+        packed,
+        ("wide", "narrow"),
+        split_axis=0,
+        concat_axis=0,
+        axis_index_groups=[group[::-1] for group in order],
+    )
+    own = own.reshape(devices // 2 * rows, LANES)
+    other = lax.ppermute(own, "wide", [(w, w ^ 1) for w in range(wide_count)])
     slots = wide_count * CAP
     return pl.pallas_call(
         functools.partial(move_kernel, rows, narrow_count, features),
@@ -191,10 +205,10 @@
             jax.ShapeDtypeStruct((3, slots), jnp.float32),
             jax.ShapeDtypeStruct((features, slots), jnp.float32),
         ),
-        in_specs=[vmem],
+        in_specs=[vmem] * 2,
         out_specs=(vmem, vmem),
         compiler_params=pltpu.CompilerParams(vmem_limit_bytes=16 << 20),
-    )(gathered)
+    )(own, other)
 
 
 def solution(mesh):

time: 17.2 us -> 16.2 us (0.942)
  blocking collectives: 14.2 us -> 12 us
  waiting for transfers between devices: 0 us -> 1.2 us
    all_to_all x1, blocking collectives: 14.2 us -> 12 us  [body(): lax.all_to_all(packed, ('wide', 'narrow'), split_axis=0, concat_axis=0, a...]
    ppermute x0 -> x1, waiting for transfers between devices: none -> 1.2 us  [body(): other = lax.ppermute(own, 'wide', [(w, w ^ 1) for w in range(wide_count)])]
  transfers between devices with their start and end apart: 0 -> 1, of which waited for: 0 -> 1; matrix products, arithmetic and copies ran while one was open for 0% -> 0% of each run, Pallas kernels for 0% -> 0%
where the time goes in v5:
time: 16.2 us; the launch traced here: 16 us
  blocking collectives  12 us (74%)
  Pallas kernels  1.48 us (9%)
  waiting for transfers between devices  1.2 us (7%)
  other arithmetic  0.68 us (4%)
  between operations  0.65 us (4%)
    all_to_all x1, blocking collectives, body(): lax.all_to_all(packed, ('wide', 'narrow'), split_axis=0, concat_axis=0, a...  12 us
    pallas_call x1, Pallas kernels, body(): pl.pallas_call(functools.partial(move_kernel, rows, narrow_count, feature...  1.26 us
    ppermute x1, waiting for transfers between devices, body(): other = lax.ppermute(own, 'wide', [(w, w ^ 1) for w in range(wide_count)])  1.2 us
    convert_element_type x1, other arithmetic, body(): small = jnp.concatenate([positions.T, owner.astype(jnp.float32)], axis=1).T  0.67 us
  transfers between devices with their start and end apart: 1, of which 1 were waited for; matrix products, arithmetic and copies ran while one was open for 0% of the time, Pallas kernels for 0%

profile of v5, /device:TPU:0, one launch (start us, length us, event | category | flops | bytes accessed | tf_op | source)
XLA Modules:
  0.0 16.0 jit_solution(1281403704352981434)
XLA Ops:
  0.6 0.0 copy-start.1
  0.6 0.0 copy-start
  0.6 0.7 %convert_element_type.3 = f32[16,1]{0,1:T(1,128)S(1)} convert(s32[16,1]{0,1:T(1,128)} %param.5) | non-fusion elementwise | flops 16 | bytes 128 | tf_op jit(solution)/shard_map/convert_element_type | solution.py:180
  1.3 0.0 copy-done.1
  1.3 0.0 copy-done
  1.3 0.2 %shard_map.50 = f32[16,4,128]{2,1,0:T(4,128)S(1)} custom-call(f32[4,16]{1,0:T(4,128)S(1)} %maximum_bitcast_fusion.small, f32[16,27]{1,0:T(8,128)S(1)} %bitcast.7), custom_call_target="tpu_custom_call" | custom-call | tf_op jit(solution)/shard_map/pallas_call | solution.py:181
  1.6 12.0 %all_to_all.5 = f32[16,4,128]{2,1,0:T(4,128)S(1)} all-to-all(f32[16,4,128]{2,1,0:T(4,128)S(1)} %shard_map.50), channel_id=1, replica_groups={{29,28,25,24,21,20,17,16,13,12,9,8,5,4,1,0},{31,30,27,26,23,22,19,18,15..., dimensions={0} | all-to-all | bytes 65536 | tf_op jit(solution)/shard_map/all_to_all | solution.py:192
  13.5 0.0 collective-permute-start
  13.5 1.2 %collective-permute-done.other = f32[64,128]{1,0:T(8,128)S(1)} collective-permute-done((f32[64,128]{1,0:T(8,128)S(1)}, f32[64,128]{1,0:T(8,128)S(1)}, u32[]{:S(2)}, u32[]{:S(2)}) %collective-permute-start) | collective-permute-done | bytes 32800 | tf_op jit(solution)/shard_map/ppermute | solution.py:200
  14.7 1.3 %shard_map.51 = (f32[3,32]{1,0:T(4,128)}, f32[27,32]{1,0:T(8,128)}) custom-call(f32[64,128]{1,0:T(8,128)S(1)} %bitcast.6, f32[64,128]{1,0:T(8,128)S(1)} %collective-permute-done.other), custom_call_target="tpu_custom_call" | custom-call | tf_op jit(solution)/shard_map/pallas_call | solution.py:202
  (1 shorter events, 0.0 us)
Async XLA Ops:
  0.6 0.7 %copy-start.1 = (f32[3,16]{1,0:T(4,128)S(1)}, f32[3,16]{1,0:T(4,128)}, u32[]{:S(2)}) copy-start(f32[3,16]{1,0:T(4,128)} %param.3) | copy-start | bytes 580
  0.6 0.7 %copy-start = (f32[27,16]{0,1:T(8,128)S(1)}, f32[27,16]{0,1:T(8,128)}, u32[]{:S(2)}) copy-start(f32[27,16]{0,1:T(8,128)} %param.4) | copy-start | bytes 5188
  13.5 1.2 %collective-permute-start = (f32[64,128]{1,0:T(8,128)S(1)}, f32[64,128]{1,0:T(8,128)S(1)}, u32[]{:S(2)}, u32[]{:S(2)}) collective-permute-start(f32[64,128]{1,0:T(8,128)S(1)} %bitcast.5), channel_id=1, source_target_pairs={{0,2},{2,0},{4,6},{6,4},{8,10},{10,8},{12,14},{14,12},{16,18},{18,... | collective-permute-start | bytes 98312 | tf_op jit(solution)/shard_map/ppermute | solution.py:200

commit v6 on v5

--- a/solution.py
+++ b/solution.py
@@ -51,6 +51,10 @@
     for g in range(1, LANES // WIDTH):
         packed = packed + pltpu.roll(wide, g * WIDTH, 1)[g * rows : (g + 1) * rows]
     out[...] = jnp.broadcast_to(packed[None], out.shape)
+
+
+def part_of(wide, wide_count):
+    return (wide + 2 * wide // wide_count) % 2
 
 
 def halves(value):
@@ -70,12 +74,15 @@
     mine_narrow = lax.axis_index("narrow")
     shape = (targets, LANES)
     slot = lax.broadcasted_iota(jnp.int32, shape, 0)
-    lane = lax.broadcasted_iota(jnp.int32, shape, 1)
     giver = slot // CAP
     source = side - 1 - giver // 2 * narrow_count - mine_narrow
-    source = source + jnp.where(giver % 2 == index % 2, 0, side)
+    wide_count = targets // CAP
+    same = part_of(giver, wide_count) == part_of(index, wide_count)
+    source = source + jnp.where(same, 0, side)
+    wanted = (source * CAP + slot % CAP).astype(jnp.float32)
+    lane = lax.broadcasted_iota(jnp.int32, (1, LANES), 1)
     device = lane // half * side + lane % half // rows
-    rank = (slot % CAP).astype(jnp.float32)
+    device = (device * CAP).astype(jnp.float32)
 
     def turned(chunk):
         at = pl.ds(chunk * half, half)
@@ -88,24 +95,24 @@
     def over(body, start):
         return body(0, start) if chunks == 1 else lax.fori_loop(0, chunks, body, start)
 
+    nobody = -1e4
+
     def collect(chunk, carry):
         block = turned(chunk)
-        here = device + chunk * (half // rows) == source
-        carry = list(carry)
+        here = device + jnp.float32(chunk * (half // rows) * CAP)
         for g in range(groups):
-            hit = (
-                here
-                & (field(block, g, features + 3) == mine_wide)
-                & (field(block, g, features + 4) == rank)
-            )
-            for c in range(3):
-                carry[c] = carry[c] + jnp.where(hit, field(block, g, features + c), 0.0)
-            carry[3] = carry[3] + jnp.where(hit, 1.0, 0.0)
-        return tuple(carry)
-
-    centre = over(collect, (jnp.zeros(shape, jnp.float32),) * 4)
-    centre = [jnp.sum(part, axis=1, keepdims=True) for part in centre]
-    valid = centre.pop() > 0.0
+            held = here + field(block, g, features + 4)
+            held = jnp.where(field(block, g, features + 3) == mine_wide, held, -1.0)
+            hit = held == wanted
+            carry = tuple(
+                jnp.maximum(carry[c], jnp.where(hit, field(block, g, features + c), nobody))
+                for c in range(3)
+            )
+        return carry
+
+    centre = over(collect, (jnp.full(shape, nobody, jnp.float32),) * 3)
+    centre = [jnp.max(part, axis=1, keepdims=True) for part in centre]
+    valid = centre[0] > 0.5 * nobody
 
     def pairs(chunk, total):
         block = turned(chunk)
@@ -186,8 +193,13 @@
         compiler_params=pltpu.CompilerParams(vmem_limit_bytes=4 << 20),
     )(small, forces.T)
     order = [
-        [w * narrow_count + n for w in range(parity, wide_count, 2) for n in range(narrow_count)]
-        for parity in range(2)
+        [
+            w * narrow_count + n
+            for w in range(wide_count)
+            for n in range(narrow_count)
+            if part_of(w, wide_count) == part
+        ]
+        for part in range(2)
     ]
     own = lax.all_to_all(
         packed,

time: 16.2 us -> 15.7 us (0.969)
  blocking collectives: 12 us -> 11.3 us
  starting transfers between devices: 0.01 us -> 0.49 us
  waiting for transfers between devices: 1.2 us -> 0.86 us
    all_to_all x1, blocking collectives: 12 us -> 11.3 us  [body(): lax.all_to_all(packed, ('wide', 'narrow'), split_axis=0, concat_axis=0, a...]
    ppermute x1, starting transfers between devices: 0.01 us -> 0.49 us  [body(): other = lax.ppermute(own, 'wide', [(w, w ^ 1) for w in range(wide_count)])]
    ppermute x1, waiting for transfers between devices: 1.2 us -> 0.86 us  [body(): other = lax.ppermute(own, 'wide', [(w, w ^ 1) for w in range(wide_count)])]
where the time goes in v6:
time: 15.7 us; the launch traced here: 15.5 us
  blocking collectives  11.3 us (72%)
  Pallas kernels  1.47 us (9%)
  waiting for transfers between devices  0.86 us (5%)
  other arithmetic  0.68 us (4%)
  between operations  0.65 us (4%)
  starting transfers between devices  0.49 us (3%)
    all_to_all x1, blocking collectives, body(): lax.all_to_all(packed, ('wide', 'narrow'), split_axis=0, concat_axis=0, a...  11.3 us
    pallas_call x1, Pallas kernels, body(): pl.pallas_call(functools.partial(move_kernel, rows, narrow_count, feature...  1.25 us
    ppermute x1, waiting for transfers between devices, body(): other = lax.ppermute(own, 'wide', [(w, w ^ 1) for w in range(wide_count)])  0.86 us
    convert_element_type x1, other arithmetic, body(): small = jnp.concatenate([positions.T, owner.astype(jnp.float32)], axis=1).T  0.67 us
    ppermute x1, starting transfers between devices, body(): other = lax.ppermute(own, 'wide', [(w, w ^ 1) for w in range(wide_count)])  0.49 us
  transfers between devices with their start and end apart: 1, of which 1 were waited for; matrix products, arithmetic and copies ran while one was open for 0% of the time, Pallas kernels for 0%

profile of v6, /device:TPU:0, one launch (start us, length us, event | category | flops | bytes accessed | tf_op | source)
XLA Modules:
  0.0 15.5 jit_solution(9755887631839314854)
XLA Ops:
  0.6 0.0 copy-start.1
  0.6 0.0 copy-start
  0.6 0.7 %convert_element_type.3 = f32[16,1]{0,1:T(1,128)S(1)} convert(s32[16,1]{0,1:T(1,128)} %param.5) | non-fusion elementwise | flops 16 | bytes 128 | tf_op jit(solution)/shard_map/convert_element_type | solution.py:187
  1.3 0.0 copy-done.1
  1.3 0.0 copy-done
  1.3 0.2 %shard_map.50 = f32[16,4,128]{2,1,0:T(4,128)S(1)} custom-call(f32[4,16]{1,0:T(4,128)S(1)} %maximum_bitcast_fusion.small, f32[16,27]{1,0:T(8,128)S(1)} %bitcast.7), custom_call_target="tpu_custom_call" | custom-call | tf_op jit(solution)/shard_map/pallas_call | solution.py:188
  1.6 11.3 %all_to_all.5 = f32[16,4,128]{2,1,0:T(4,128)S(1)} all-to-all(f32[16,4,128]{2,1,0:T(4,128)S(1)} %shard_map.50), channel_id=1, replica_groups={{31,30,27,26,23,22,19,18,13,12,9,8,5,4,1,0},{29,28,25,24,21,20,17,16,15..., dimensions={0} | all-to-all | bytes 65536 | tf_op jit(solution)/shard_map/all_to_all | solution.py:204
  12.9 0.5 %collective-permute-start = (f32[64,128]{1,0:T(8,128)S(1)}, f32[64,128]{1,0:T(8,128)S(1)}, u32[]{:S(2)}, u32[]{:S(2)}) collective-permute-start(f32[64,128]{1,0:T(8,128)S(1)} %bitcast.5), channel_id=1, source_target_pairs={{0,2},{2,0},{4,6},{6,4},{8,10},{10,8},{12,14},{14,12},{16,18},{18,... | collective-permute-start | bytes 98312 | tf_op jit(solution)/shard_map/ppermute | solution.py:212
  13.4 0.9 %collective-permute-done.other = f32[64,128]{1,0:T(8,128)S(1)} collective-permute-done((f32[64,128]{1,0:T(8,128)S(1)}, f32[64,128]{1,0:T(8,128)S(1)}, u32[]{:S(2)}, u32[]{:S(2)}) %collective-permute-start) | collective-permute-done | bytes 32800 | tf_op jit(solution)/shard_map/ppermute | solution.py:212
  14.2 1.3 %shard_map.51 = (f32[3,32]{1,0:T(4,128)}, f32[27,32]{1,0:T(8,128)}) custom-call(f32[64,128]{1,0:T(8,128)S(1)} %bitcast.6, f32[64,128]{1,0:T(8,128)S(1)} %collective-permute-done.other), custom_call_target="tpu_custom_call" | custom-call | tf_op jit(solution)/shard_map/pallas_call | solution.py:214
  (1 shorter events, 0.0 us)
Async XLA Ops:
  0.6 0.7 %copy-start.1 = (f32[3,16]{1,0:T(4,128)S(1)}, f32[3,16]{1,0:T(4,128)}, u32[]{:S(2)}) copy-start(f32[3,16]{1,0:T(4,128)} %param.3) | copy-start | bytes 580
  0.6 0.7 %copy-start = (f32[27,16]{0,1:T(8,128)S(1)}, f32[27,16]{0,1:T(8,128)}, u32[]{:S(2)}) copy-start(f32[27,16]{0,1:T(8,128)} %param.4) | copy-start | bytes 5188
  12.9 1.3 %collective-permute-start = (f32[64,128]{1,0:T(8,128)S(1)}, f32[64,128]{1,0:T(8,128)S(1)}, u32[]{:S(2)}, u32[]{:S(2)}) collective-permute-start(f32[64,128]{1,0:T(8,128)S(1)} %bitcast.5), channel_id=1, source_target_pairs={{0,2},{2,0},{4,6},{6,4},{8,10},{10,8},{12,14},{14,12},{16,18},{18,... | collective-permute-start | bytes 98312 | tf_op jit(solution)/shard_map/ppermute | solution.py:212

commit v7 on v6

--- a/solution.py
+++ b/solution.py
@@ -53,8 +53,11 @@
     out[...] = jnp.broadcast_to(packed[None], out.shape)
 
 
-def part_of(wide, wide_count):
-    return (wide + 2 * wide // wide_count) % 2
+LAYER = 4
+
+
+def part_of(wide):
+    return (wide + wide // LAYER) % 2
 
 
 def halves(value):
@@ -75,10 +78,10 @@
     shape = (targets, LANES)
     slot = lax.broadcasted_iota(jnp.int32, shape, 0)
     giver = slot // CAP
-    source = side - 1 - giver // 2 * narrow_count - mine_narrow
-    wide_count = targets // CAP
-    same = part_of(giver, wide_count) == part_of(index, wide_count)
-    source = source + jnp.where(same, 0, side)
+    part = part_of(giver)
+    source = side - 1 - giver // 2 * narrow_count - mine_narrow - part * (LAYER // 2 * narrow_count)
+    source = jnp.where(source < 0, source + side, source)
+    source = source + jnp.where(part == part_of(index), 0, side)
     wanted = (source * CAP + slot % CAP).astype(jnp.float32)
     lane = lax.broadcasted_iota(jnp.int32, (1, LANES), 1)
     device = lane // half * side + lane % half // rows
@@ -197,16 +200,18 @@
             w * narrow_count + n
             for w in range(wide_count)
             for n in range(narrow_count)
-            if part_of(w, wide_count) == part
+            if part_of(w) == part
         ]
         for part in range(2)
     ]
+    layer = LAYER // 2 * narrow_count
+    order = [order[0][::-1], order[1][: -layer][::-1] + order[1][-layer:][::-1]]
     own = lax.all_to_all(
         packed,
         ("wide", "narrow"),
         split_axis=0,
         concat_axis=0,
-        axis_index_groups=[group[::-1] for group in order],
+        axis_index_groups=order,
     )
     own = own.reshape(devices // 2 * rows, LANES)
     other = lax.ppermute(own, "wide", [(w, w ^ 1) for w in range(wide_count)])

time: 15.7 us -> 15.5 us (0.987)
  starting transfers between devices: 0.49 us -> 0.33 us
    ppermute x1, starting transfers between devices: 0.49 us -> 0.33 us  [body(): other = lax.ppermute(own, 'wide', [(w, w ^ 1) for w in range(wide_count)])]
where the time goes in v7:
time: 15.5 us; the launch traced here: 15.3 us
  blocking collectives  11.3 us (73%)
  Pallas kernels  1.48 us (10%)
  waiting for transfers between devices  0.88 us (6%)
  other arithmetic  0.68 us (4%)
  between operations  0.65 us (4%)
  starting transfers between devices  0.33 us (2%)
    all_to_all x1, blocking collectives, body(): lax.all_to_all(packed, ('wide', 'narrow'), split_axis=0, concat_axis=0, a...  11.3 us
    pallas_call x1, Pallas kernels, body(): pl.pallas_call(functools.partial(move_kernel, rows, narrow_count, feature...  1.26 us
    ppermute x1, waiting for transfers between devices, body(): other = lax.ppermute(own, 'wide', [(w, w ^ 1) for w in range(wide_count)])  0.88 us
    convert_element_type x1, other arithmetic, body(): small = jnp.concatenate([positions.T, owner.astype(jnp.float32)], axis=1).T  0.67 us
    ppermute x1, starting transfers between devices, body(): other = lax.ppermute(own, 'wide', [(w, w ^ 1) for w in range(wide_count)])  0.33 us
  transfers between devices with their start and end apart: 1, of which 1 were waited for; matrix products, arithmetic and copies ran while one was open for 0% of the time, Pallas kernels for 0%

profile of v7, /device:TPU:0, one launch (start us, length us, event | category | flops | bytes accessed | tf_op | source)
XLA Modules:
  0.0 15.3 jit_solution(6794675477395054264)
XLA Ops:
  0.6 0.0 copy-start.1
  0.6 0.0 copy-start
  0.6 0.7 %convert_element_type.3 = f32[16,1]{0,1:T(1,128)S(1)} convert(s32[16,1]{0,1:T(1,128)} %param.5) | non-fusion elementwise | flops 16 | bytes 128 | tf_op jit(solution)/shard_map/convert_element_type | solution.py:190
  1.3 0.0 copy-done.1
  1.3 0.0 copy-done
  1.3 0.2 %shard_map.50 = f32[16,4,128]{2,1,0:T(4,128)S(1)} custom-call(f32[4,16]{1,0:T(4,128)S(1)} %maximum_bitcast_fusion.small, f32[16,27]{1,0:T(8,128)S(1)} %bitcast.7), custom_call_target="tpu_custom_call" | custom-call | tf_op jit(solution)/shard_map/pallas_call | solution.py:191
  1.6 11.3 %all_to_all.5 = f32[16,4,128]{2,1,0:T(4,128)S(1)} all-to-all(f32[16,4,128]{2,1,0:T(4,128)S(1)} %shard_map.50), channel_id=1, replica_groups={{31,30,27,26,21,20,17,16,15,14,11,10,5,4,1,0},{23,22,19,18,13,12,9,8,7,..., dimensions={0} | all-to-all | bytes 65536 | tf_op jit(solution)/shard_map/all_to_all | solution.py:209
  12.8 0.3 %collective-permute-start = (f32[64,128]{1,0:T(8,128)S(1)}, f32[64,128]{1,0:T(8,128)S(1)}, u32[]{:S(2)}, u32[]{:S(2)}) collective-permute-start(f32[64,128]{1,0:T(8,128)S(1)} %bitcast.5), channel_id=1, source_target_pairs={{0,2},{2,0},{4,6},{6,4},{8,10},{10,8},{12,14},{14,12},{16,18},{18,... | collective-permute-start | bytes 98312 | tf_op jit(solution)/shard_map/ppermute | solution.py:217
  13.1 0.9 %collective-permute-done.other = f32[64,128]{1,0:T(8,128)S(1)} collective-permute-done((f32[64,128]{1,0:T(8,128)S(1)}, f32[64,128]{1,0:T(8,128)S(1)}, u32[]{:S(2)}, u32[]{:S(2)}) %collective-permute-start) | collective-permute-done | bytes 32800 | tf_op jit(solution)/shard_map/ppermute | solution.py:217
  14.0 1.3 %shard_map.51 = (f32[3,32]{1,0:T(4,128)}, f32[27,32]{1,0:T(8,128)}) custom-call(f32[64,128]{1,0:T(8,128)S(1)} %bitcast.6, f32[64,128]{1,0:T(8,128)S(1)} %collective-permute-done.other), custom_call_target="tpu_custom_call" | custom-call | tf_op jit(solution)/shard_map/pallas_call | solution.py:219
  (1 shorter events, 0.0 us)
Async XLA Ops:
  0.6 0.7 %copy-start.1 = (f32[3,16]{1,0:T(4,128)S(1)}, f32[3,16]{1,0:T(4,128)}, u32[]{:S(2)}) copy-start(f32[3,16]{1,0:T(4,128)} %param.3) | copy-start | bytes 580
  0.6 0.7 %copy-start = (f32[27,16]{0,1:T(8,128)S(1)}, f32[27,16]{0,1:T(8,128)}, u32[]{:S(2)}) copy-start(f32[27,16]{0,1:T(8,128)} %param.4) | copy-start | bytes 5188
  12.8 1.2 %collective-permute-start = (f32[64,128]{1,0:T(8,128)S(1)}, f32[64,128]{1,0:T(8,128)S(1)}, u32[]{:S(2)}, u32[]{:S(2)}) collective-permute-start(f32[64,128]{1,0:T(8,128)S(1)} %bitcast.5), channel_id=1, source_target_pairs={{0,2},{2,0},{4,6},{6,4},{8,10},{10,8},{12,14},{14,12},{16,18},{18,... | collective-permute-start | bytes 98312 | tf_op jit(solution)/shard_map/ppermute | solution.py:217
